TPU v7x, 256 devices: a whole 4x4x8 slice. The times are simulated.
256 devices in a mesh: wide: 32 (over x, y, core), narrow: 8 (over z).
Axes of the slice: x: 4, y: 4, z: 8, core: 2. Of those that a mesh axis runs over, the one named last changes fastest.
Arguments:
- design: float32 [262144, 256], P(('wide', 'narrow')), as said below
- sign_flips: int32 [262144], P(('wide', 'narrow')), may hold values from -1 to 1, as said below
- sample_ids: int32 [1024], replicated, may hold values from 0 to 262143
Outputs:
- sketch: float32 [1024, 256], P(('wide', 'narrow'))
- gram_matrix: float32 [256, 256], replicated
Inputs may be any that keep to these rules, and one draw needn't show every extreme that they name: `sign_flips`: each entry is +1 or -1. `design`: real-valued entries of varying row and column scales.
All inputs are finite; a program needn't handle non-finite values.
Results may differ from a plain program's by a relative error of at most 0.00012.
Values sent between devices are 32-bit elements; how exact they have to be, the bound alone decides.
A program may use at most 64 MiB of HBM per device.

v0:
```python
import math

import jax
import jax.numpy as jnp
from jax import lax
from jax.sharding import PartitionSpec as P


def swapped(x, axis, distance):
    return lax.ppermute(x, axis, [(i, i ^ 1 << distance) for i in range(lax.axis_size(axis))])


def parity(values, nbits):
    counted = jnp.zeros_like(values)
    for level in range(nbits):
        counted = counted + (jnp.right_shift(values, level) & 1)
    return counted & 1


def sign_table(row_ids, col_ids, nbits):
    bits_both = row_ids[:, None] & col_ids[None, :]
    return (1 - 2 * parity(bits_both, nbits)).astype(jnp.float32)


def on_device(design, sign_flips, sample_ids):
    local_rows, features = design.shape
    wide_count = lax.axis_size("wide")
    narrow_count = lax.axis_size("narrow")
    dev_count = wide_count * narrow_count
    total_rows = local_rows * dev_count
    samples_all = sample_ids.shape[0]
    scale = 1.0 / math.sqrt(total_rows)
    my_wide = lax.axis_index("wide")
    my_narrow = lax.axis_index("narrow")
    my_device = my_wide * narrow_count + my_narrow
    highest = lax.Precision.HIGHEST
    flipped = design * sign_flips.astype(jnp.float32)[:, None]
    outer = local_rows // 128
    inner_ids = jnp.arange(128, dtype=jnp.int32)
    outer_ids = jnp.arange(outer, dtype=jnp.int32)
    inner_table = sign_table(inner_ids, inner_ids, 7)
    outer_table = sign_table(outer_ids, outer_ids, max(outer.bit_length() - 1, 0))
    blocks = flipped.reshape(outer, 128, features)
    blocks = jnp.einsum("ap,qpd->qad", inner_table, blocks, precision=highest)
    blocks = jnp.einsum("bq,qad->bad", outer_table, blocks, precision=highest)
    mixing = blocks.reshape(local_rows, features)
    narrow_bits = narrow_count.bit_length() - 1
    for level in range(narrow_bits):
        partner = swapped(mixing, "narrow", level)
        upper = jnp.right_shift(my_narrow, level) & 1 == 1
        mixing = jnp.where(upper, partner - mixing, mixing + partner)
    wide_bits = wide_count.bit_length() - 1
    for level in range(wide_bits):
        partner = swapped(mixing, "wide", level)
        upper = jnp.right_shift(my_wide, level) & 1 == 1
        mixing = jnp.where(upper, partner - mixing, mixing + partner)
    owned = sample_ids // local_rows == my_device
    place = sample_ids % local_rows
    place = jnp.where(owned, place, 0)
    weight = jnp.where(owned, scale, 0.0).astype(jnp.float32)
    sketch = lax.psum_scatter(
        jnp.take(mixing, place, axis=0) * weight[:, None],
        ("wide", "narrow"),
        scatter_dimension=0,
        tiled=True,
    )
    own_term = jnp.dot(sketch.T, sketch, precision=highest)
    gram_matrix = lax.psum(own_term, ("wide", "narrow")) / samples_all
    return (sketch, gram_matrix)


def solution(mesh):
    placed = (P(("wide", "narrow"), None), P(("wide", "narrow")), P())
    return jax.shard_map(
        on_device,
        mesh=mesh,
        in_specs=placed,
        out_specs=(P(("wide", "narrow"), None), P()),
        check_vma=False,
    )
```

profile of v0, /device:TPU:1, one launch (start us, length us, event | category | flops | bytes accessed | tf_op | source)
XLA Modules:
  0.0 764.8 jit_solution(15457126658020371489)
XLA Ops:
  7.2 0.0 all-reduce.6.cloned.1.call-start
  7.2 0.7 convert_element_type.10
  7.9 1.4 broadcast_multiply_fusion
  9.3 1.8 convolution_bitcast_fusion
  11.1 0.5 copy.7
  11.6 1.0 fusion.37
  12.6 0.3 copy.8
  13.0 2.6 collective-permute-start
  15.5 21.8 %collective-permute-done = f32[1024,256]{1,0:T(8,128)S(1)} collective-permute-done((f32[1024,256]{1,0:T(8,128)S(1)}, f32[1024,256]{1,0:T(8,128)S(1)}, u32[]{:S(2)}, u32[]{:S(2)}) %collective-permute-start) | collective-permute-done | bytes 1048608 | tf_op jit(solution)/shard_map/ppermute | solution.py:10
  37.3 0.1 add_select_fusion.7
  37.5 4.0 collective-permute-start.1
  41.5 45.0 %collective-permute-done.1 = f32[1024,256]{1,0:T(8,128)S(1)} collective-permute-done((f32[1024,256]{1,0:T(8,128)S(1)}, f32[1024,256]{1,0:T(8,128)S(1)}, u32[]{:S(2)}, u32[]{:S(2)}) %collective-permute-start.1) | collective-permute-done | bytes 1048608 | tf_op jit(solution)/shard_map/ppermute | solution.py:10
  86.5 0.1 add_select_fusion.6
  86.7 6.5 collective-permute-start.2
  93.2 45.4 %collective-permute-done.2 = f32[1024,256]{1,0:T(8,128)S(1)} collective-permute-done((f32[1024,256]{1,0:T(8,128)S(1)}, f32[1024,256]{1,0:T(8,128)S(1)}, u32[]{:S(2)}, u32[]{:S(2)}) %collective-permute-start.2) | collective-permute-done | bytes 1048608 | tf_op jit(solution)/shard_map/ppermute | solution.py:10
  138.6 0.1 add_select_fusion.5
  138.7 1.8 collective-permute-start.3
  140.5 2.3 collective-permute-done.3
  142.8 0.1 add_select_fusion.4
  142.9 1.4 collective-permute-start.4
  144.3 23.1 %collective-permute-done.4 = f32[1024,256]{1,0:T(8,128)S(1)} collective-permute-done((f32[1024,256]{1,0:T(8,128)S(1)}, f32[1024,256]{1,0:T(8,128)S(1)}, u32[]{:S(2)}, u32[]{:S(2)}) %collective-permute-start.4) | collective-permute-done | bytes 1048608 | tf_op jit(solution)/shard_map/ppermute | solution.py:10
  167.4 0.1 add_select_fusion.3
  167.5 3.0 collective-permute-start.5
  170.5 22.0 %collective-permute-done.5 = f32[1024,256]{1,0:T(8,128)S(1)} collective-permute-done((f32[1024,256]{1,0:T(8,128)S(1)}, f32[1024,256]{1,0:T(8,128)S(1)}, u32[]{:S(2)}, u32[]{:S(2)}) %collective-permute-start.5) | collective-permute-done | bytes 1048608 | tf_op jit(solution)/shard_map/ppermute | solution.py:10
  192.5 0.1 add_select_fusion.2
  192.7 1.3 collective-permute-start.6
  194.0 21.3 %collective-permute-done.6 = f32[1024,256]{1,0:T(8,128)S(1)} collective-permute-done((f32[1024,256]{1,0:T(8,128)S(1)}, f32[1024,256]{1,0:T(8,128)S(1)}, u32[]{:S(2)}, u32[]{:S(2)}) %collective-permute-start.6) | collective-permute-done | bytes 1048608 | tf_op jit(solution)/shard_map/ppermute | solution.py:10
  215.3 0.1 add_select_fusion.1
  215.4 2.8 collective-permute-start.7
  218.3 0.0 copy-start.1
  218.3 0.7 copy-done.1
  219.0 20.4 %collective-permute-done.7 = f32[1024,256]{1,0:T(8,128)S(1)} collective-permute-done((f32[1024,256]{1,0:T(8,128)S(1)}, f32[1024,256]{1,0:T(8,128)S(1)}, u32[]{:S(2)}, u32[]{:S(2)}) %collective-permute-start.7) | collective-permute-done | bytes 1048608 | tf_op jit(solution)/shard_map/ppermute | solution.py:10
  239.4 0.1 add_select_fusion
  239.6 3.5 gather_fusion
  243.0 1.3 select_multiply_fusion
  244.4 0.0 all-reduce.6.cloned.1.call-update
  244.4 0.0 all-reduce.4.cloned.1.call-start
  244.5 255.8 %all-reduce.6.cloned.1.call-done = f32[1024,256]{1,0:T(8,128)} async-done(((f32[1024,256]{1,0:T(8,128)}), f32[1024,256]{1,0:T(8,128)}) %all-reduce.6.cloned.1.call-update) | async-done | bytes 1048592
  500.3 0.7 constant_dynamic-slice_fusion
  501.0 0.0 copy-start
  501.0 1.1 fusion.70
  502.1 0.0 copy-done
  502.1 0.0 all-reduce.4.cloned.1.call-update
  502.2 254.2 %all-reduce.4.cloned.1.call-done = f32[256,256]{1,0:T(8,128)} async-done(((f32[256,256]{1,0:T(8,128)}), f32[256,256]{1,0:T(8,128)}) %all-reduce.4.cloned.1.call-update) | async-done | bytes 262160 | tf_op jit(solution)/shard_map/psum | solution.py:68
  756.3 1.7 broadcast_multiply_fusion.1
  (3 shorter events, 0.0 us)
Async XLA Ops:
  7.2 493.1 %all-reduce.6.cloned.1.call-start = ((), (), s32[]{:S(2)}) async-start(), calls=%async_computation.1 | async-start | bytes 2097152
  13.0 24.4 %collective-permute-start = (f32[1024,256]{1,0:T(8,128)S(1)}, f32[1024,256]{1,0:T(8,128)S(1)}, u32[]{:S(2)}, u32[]{:S(2)}) collective-permute-start(f32[1024,256]{1,0:T(8,128)S(1)} %bitcast.15), channel_id=1, source_target_pairs={{0,1},{1,0},{2,3},{3,2},{4,5},{5,4},{6,7},{7,6},{8,9},{9,8},{10,11... | collective-permute-start | bytes 3145736 | tf_op jit(solution)/shard_map/ppermute | solution.py:10
  37.5 49.1 %collective-permute-start.1 = (f32[1024,256]{1,0:T(8,128)S(1)}, f32[1024,256]{1,0:T(8,128)S(1)}, u32[]{:S(2)}, u32[]{:S(2)}) collective-permute-start(f32[1024,256]{1,0:T(8,128)S(1)} %add_select_fusion.7), channel_id=1, source_target_pairs={{0,2},{1,3},{2,0},{3,1},{4,6},{5,7},{6,4},{7,5},{8,10},{9,11},{10,... | collective-permute-start | bytes 3145736 | tf_op jit(solution)/shard_map/ppermute | solution.py:10
  86.7 51.9 %collective-permute-start.2 = (f32[1024,256]{1,0:T(8,128)S(1)}, f32[1024,256]{1,0:T(8,128)S(1)}, u32[]{:S(2)}, u32[]{:S(2)}) collective-permute-start(f32[1024,256]{1,0:T(8,128)S(1)} %add_select_fusion.6), channel_id=1, source_target_pairs={{0,4},{1,5},{2,6},{3,7},{4,0},{5,1},{6,2},{7,3},{8,12},{9,13},{10,... | collective-permute-start | bytes 3145736 | tf_op jit(solution)/shard_map/ppermute | solution.py:10
  138.7 4.0 collective-permute-start.3
  142.9 24.5 %collective-permute-start.4 = (f32[1024,256]{1,0:T(8,128)S(1)}, f32[1024,256]{1,0:T(8,128)S(1)}, u32[]{:S(2)}, u32[]{:S(2)}) collective-permute-start(f32[1024,256]{1,0:T(8,128)S(1)} %add_select_fusion.4), channel_id=1, source_target_pairs={{0,16},{8,24},{16,0},{24,8},{32,48},{40,56},{48,32},{56,40},{64,80... | collective-permute-start | bytes 3145736 | tf_op jit(solution)/shard_map/ppermute | solution.py:10
  167.5 25.0 %collective-permute-start.5 = (f32[1024,256]{1,0:T(8,128)S(1)}, f32[1024,256]{1,0:T(8,128)S(1)}, u32[]{:S(2)}, u32[]{:S(2)}) collective-permute-start(f32[1024,256]{1,0:T(8,128)S(1)} %add_select_fusion.3), channel_id=1, source_target_pairs={{0,32},{8,40},{16,48},{24,56},{32,0},{40,8},{48,16},{56,24},{64,96... | collective-permute-start | bytes 3145736 | tf_op jit(solution)/shard_map/ppermute | solution.py:10
  192.7 22.6 %collective-permute-start.6 = (f32[1024,256]{1,0:T(8,128)S(1)}, f32[1024,256]{1,0:T(8,128)S(1)}, u32[]{:S(2)}, u32[]{:S(2)}) collective-permute-start(f32[1024,256]{1,0:T(8,128)S(1)} %add_select_fusion.2), channel_id=1, source_target_pairs={{0,64},{8,72},{16,80},{24,88},{32,96},{40,104},{48,112},{56,120},{... | collective-permute-start | bytes 3145736 | tf_op jit(solution)/shard_map/ppermute | solution.py:10
  215.4 24.0 %collective-permute-start.7 = (f32[1024,256]{1,0:T(8,128)S(1)}, f32[1024,256]{1,0:T(8,128)S(1)}, u32[]{:S(2)}, u32[]{:S(2)}) collective-permute-start(f32[1024,256]{1,0:T(8,128)S(1)} %add_select_fusion.1), channel_id=1, source_target_pairs={{0,128},{8,136},{16,144},{24,152},{32,160},{40,168},{48,176},{56,1... | collective-permute-start | bytes 3145736 | tf_op jit(solution)/shard_map/ppermute | solution.py:10
  218.3 0.7 copy-start.1
  244.4 511.9 %all-reduce.4.cloned.1.call-start = ((), (), s32[]{:S(2)}) async-start(), calls=%async_computation | async-start | bytes 524288 | tf_op jit(solution)/shard_map/psum | solution.py:68
  501.0 1.1 copy-start
Sparse Core Ops, SparseCore 0:
  244.5 255.7 all-reduce.5
  507.2 249.0 all-reduce.3
where the time goes:
time: 766 us; the launch traced here: 765 us
  waiting for transfers between devices  711 us (93%)
  starting transfers between devices  23.4 us (3%)
  between operations  14.1 us (2%)
    unnamed x3, waiting for transfers between devices  256 us
    psum x1, waiting for transfers between devices, on_device(): gram_matrix = lax.psum(own_term, ('wide', 'narrow')) / samples_all  254 us
    ppermute x8, waiting for transfers between devices, swapped(): lax.ppermute(x, axis, [(i, i ^ 1 << distance) for i in range(lax.axis_siz...  201 us
    ppermute x8, starting transfers between devices, swapped(): lax.ppermute(x, axis, [(i, i ^ 1 << distance) for i in range(lax.axis_siz...  23.3 us
  transfers between devices with their start and end apart: 10, of which 10 were waited for; matrix products, arithmetic and copies ran while one was open for 0% of the time, Pallas kernels for 0%

commit v1 on v0

v1 whole, which is shorter than its diff:
```python
import functools

import jax
import jax.numpy as jnp
from jax import lax
from jax.experimental import pallas as pl
from jax.experimental.pallas import tpu as pltpu
from jax.sharding import PartitionSpec as P

MESH = pl.DeviceIdType.MESH
FAR_FIRST = (2, 1, 3, 0)
Z_ORDER = (4, 3, 5, 2, 6, 1, 7)
BF16, F32, I32 = jnp.bfloat16, jnp.float32, jnp.int32


def contract_rows(a, b):
    return lax.dot_general(a, b, (((0,), (0,)), ((), ())), preferred_element_type=F32)


def kernel(
    design, flips, ids, sketch_out, gram_out,
    rows_in, rows_hi, rows_lo, bits, masks, part, from_sib, chip_sum,
    plane_in, plane_sum, line_in, gathered, gram_own, gram_sib,
    load_sem, sib_send, sib_recv, plane_send, plane_recv, line_send, line_recv,
    gather_send, gather_recv, gram_send, gram_recv,
):
    wide, z = lax.axis_index("wide"), lax.axis_index("narrow")
    core = lax.rem(wide, 2)
    square = lax.div(wide, 2)
    x, y = lax.div(square, 4), lax.rem(square, 4)
    device = wide * 8 + z

    load = pltpu.make_async_copy(design, rows_in, load_sem)
    load.start()

    def wrap(v, n):
        return lax.rem(v, n)

    plane = [(dx, dy) for dx in FAR_FIRST for dy in FAR_FIRST if dx or dy]

    def plane_square(dx, dy):
        return wrap(x + dx, 4) * 4 + wrap(y + dy, 4)

    sibling = (wide + 1 - 2 * core, z)
    line = [(dz, dc) for dz in Z_ORDER for dc in (0, 1)]

    barrier = pltpu.get_barrier_semaphore()
    for dz, dc in line:
        target = (square * 2 + wrap(core + dc, 2), wrap(z + dz, 8))
        pl.semaphore_signal(barrier, inc=1, device_id=target, device_id_type=MESH)
    for dx, dy in plane:
        target = (plane_square(dx, dy) * 2 + core, z)
        pl.semaphore_signal(barrier, inc=1, device_id=target, device_id_type=MESH)
    pl.semaphore_signal(barrier, inc=1, device_id=sibling, device_id_type=MESH)

    bit = lax.broadcasted_iota(I32, (32, 1024), 0)
    bits[...] = (lax.shift_right_logical(jnp.broadcast_to(ids[...], (32, 1024)), bit) & 1).astype(F32).astype(BF16)
    bit = lax.broadcasted_iota(I32, (32, 512), 0)
    lane = lax.broadcasted_iota(I32, (32, 512), 1)
    block, low = lax.shift_right_logical(lane, 7), lane & 127
    of_low = lax.shift_right_logical(low, jnp.minimum(bit, 7)) & 1
    of_device = lax.shift_right_logical(jnp.full((32, 512), device, I32), jnp.maximum(bit - 10, 0)) & 1
    of_device = jnp.where(bit >= 10, of_device, 0)
    first = jnp.where(bit < 7, of_low, of_device)
    masks[...] = jnp.where(block == 0, first, jnp.where(bit == 6 + block, 1, 0)).astype(F32).astype(BF16)

    load.wait()
    scaled = rows_in[...] * (1.0 / 512.0)
    hi = scaled.astype(BF16)
    rows_hi[...] = hi
    rows_lo[...] = (scaled - hi.astype(F32)).astype(BF16)
    flip = flips[...].astype(F32).astype(BF16)

    def local(m, _):
        span = pl.ds(pl.multiple_of(m * 256, 256), 256)
        counts = contract_rows(bits[:, span], masks[...])
        base = (1 - 2 * (counts[:, :128].astype(I32) & 1)).astype(F32).astype(BF16)
        by_bit = [(1.0 - 2.0 * counts[:, 128 * j : 128 * j + 128]).astype(BF16) for j in (1, 2, 3)]
        signs = [base]
        for j in range(3):
            signs = signs + [s * by_bit[j] for s in signs]
        signs = [s * jnp.broadcast_to(flip[:, 128 * k : 128 * k + 128], (256, 128)) for k, s in enumerate(signs)]
        table = jnp.concatenate(signs, axis=1)
        got = jnp.dot(table, rows_hi[...], preferred_element_type=F32)
        got = got + jnp.dot(table, rows_lo[...], preferred_element_type=F32)
        part[0, m] = got[:, :128]
        part[1, m] = got[:, 128:]
        return 0

    lax.fori_loop(0, 4, local, 0)
    pl.semaphore_wait(barrier, len(line) + len(plane) + 1)

    halves = []
    for k, dx in enumerate(FAR_FIRST):
        m = wrap(x + dx, 4)
        copy = pltpu.make_async_remote_copy(
            part.at[1 - core, m], from_sib.at[m], sib_send.at[k], sib_recv.at[k], device_id=sibling, device_id_type=MESH
        )
        copy.start()
        halves.append(copy)
    sent = []
    for k, dx in enumerate(FAR_FIRST):
        m = wrap(x + dx, 4)
        halves[k].wait_recv()
        chip_sum[pl.ds(m * 4, 4)] = (part[core, m] + from_sib[m]).reshape(4, 64, 128)
        for dy in FAR_FIRST:
            if dx or dy:
                there = plane_square(dx, dy)
                n = len(sent)
                copy = pltpu.make_async_remote_copy(
                    chip_sum.at[there], plane_in.at[n], plane_send.at[n], plane_recv.at[n],
                    device_id=(there * 2 + core, z), device_id_type=MESH,
                )
                copy.start()
                sent.append(copy)
    total = chip_sum[square]
    for n in reversed(range(15)):
        sent[n].wait_recv()
        total = total + plane_in[n]
    plane_sum[...] = total.reshape(2, 32, 128)

    along = []
    for n, (dz, dc) in enumerate(line + [(0, 1)]):
        to_core = wrap(core + dc, 2)
        copy = pltpu.make_async_remote_copy(
            plane_sum.at[to_core], line_in.at[z, core], line_send.at[n], line_recv.at[n],
            device_id=(square * 2 + to_core, wrap(z + dz, 8)), device_id_type=MESH,
        )
        copy.start()
        along.append(copy)
    line_in[z, core] = plane_sum[core]
    for copy in reversed(along):
        copy.wait_recv()
    for h in range(2):
        total = line_in[0, h]
        for k in range(1, 8):
            total = total + line_in[k, h]
        gathered[square, :, 128 * h : 128 * h + 128] = total

    round_sent = []
    for n, (dx, dy) in enumerate(plane):
        copy = pltpu.make_async_remote_copy(
            gathered.at[square], gathered.at[square], gather_send.at[n], gather_recv.at[n],
            device_id=(plane_square(dx, dy) * 2 + core, z), device_id_type=MESH,
        )
        copy.start()
        round_sent.append(copy)
    pair = gathered[square, pl.ds(pl.multiple_of(lax.div(z, 2) * 8, 8), 8)]
    sketch_out[...] = jnp.where(lax.rem(z, 2) == 0, pair[:4], pair[4:])
    for copy in halves + sent + along:
        copy.wait_send()
    for copy in reversed(round_sent):
        copy.wait_recv()

    rows = gathered[...].reshape(512, 256)
    hi = rows.astype(BF16)
    lo = (rows - hi.astype(F32)).astype(BF16)
    cross = contract_rows(hi, lo)
    gram = contract_rows(hi, hi) + (cross + cross.T)
    gram_own[...] = gram * (1.0 / 1024.0)
    copy = pltpu.make_async_remote_copy(
        gram_own, gram_sib, gram_send, gram_recv, device_id=sibling, device_id_type=MESH
    )
    copy.start()
    copy.wait()
    gram_out[...] = gram_own[...] + gram_sib[...]
    for copy in round_sent:
        copy.wait_send()


def on_device(design, sign_flips, sample_ids):
    dma = pltpu.SemaphoreType.DMA
    vmem = pl.BlockSpec(memory_space=pltpu.VMEM)
    return pl.pallas_call(
        kernel,
        out_shape=(jax.ShapeDtypeStruct((4, 256), F32), jax.ShapeDtypeStruct((256, 256), F32)),
        in_specs=[pl.BlockSpec(memory_space=pl.ANY), vmem, vmem],
        out_specs=(vmem, vmem),
        scratch_shapes=[
            pltpu.VMEM((1024, 256), F32),
            pltpu.VMEM((1024, 256), BF16),
            pltpu.VMEM((1024, 256), BF16),
            pltpu.VMEM((32, 1024), BF16),
            pltpu.VMEM((32, 512), BF16),
            pltpu.VMEM((2, 4, 256, 128), F32),
            pltpu.VMEM((4, 256, 128), F32),
            pltpu.VMEM((16, 64, 128), F32),
            pltpu.VMEM((15, 64, 128), F32),
            pltpu.VMEM((2, 32, 128), F32),
            pltpu.VMEM((8, 2, 32, 128), F32),
            pltpu.VMEM((16, 32, 256), F32),
            pltpu.VMEM((256, 256), F32),
            pltpu.VMEM((256, 256), F32),
            dma, dma((4,)), dma((4,)), dma((15,)), dma((15,)), dma((15,)), dma((15,)),
            dma((15,)), dma((15,)), dma, dma,
        ],
        compiler_params=pltpu.CompilerParams(collective_id=0, has_side_effects=True, vmem_limit_bytes=48 << 20),
    )(design, sign_flips.reshape(1, 1024), sample_ids.reshape(1, 1024))


def solution(mesh):
    placed = (P(("wide", "narrow"), None), P(("wide", "narrow")), P())
    return jax.shard_map(
        on_device,
        mesh=mesh,
        in_specs=placed,
        out_specs=(P(("wide", "narrow"), None), P()),
        check_vma=False,
    )
```

time: 766 us -> 44.7 us (0.06)
  waiting for transfers between devices: 711 us -> 0 us
  Pallas kernels: 0 us -> 39.9 us
  starting transfers between devices: 23.4 us -> 0 us
  between operations: 14.1 us -> 0.65 us
    unnamed x3 -> x0, waiting for transfers between devices: 256 us -> none
    psum x1 -> x0, waiting for transfers between devices: 254 us -> none  [on_device(): gram_matrix = lax.psum(own_term, ('wide', 'narrow')) / samples_all]
    ppermute x8 -> x0, waiting for transfers between devices: 201 us -> none  [swapped(): lax.ppermute(x, axis, [(i, i ^ 1 << distance) for i in range(lax.axis_siz...]
    pallas_call x0 -> x1, Pallas kernels: none -> 39.9 us  [on_device(): pl.pallas_call(kernel, out_shape=(jax.ShapeDtypeStruct((4, 256), F32), ja...]
    ppermute x8 -> x0, starting transfers between devices: 23.3 us -> none  [swapped(): lax.ppermute(x, axis, [(i, i ^ 1 << distance) for i in range(lax.axis_siz...]
  transfers between devices with their start and end apart: 10 -> 0, of which waited for: 10 -> 0; matrix products, arithmetic and copies ran while one was open for 0% -> 0% of each run, Pallas kernels for 0% -> 0%
where the time goes in v1:
time: 44.7 us; the launch traced here: 44.5 us
  Pallas kernels  39.9 us (89%)
  local copies, waits for them, and re-layouts  3.89 us (9%)
  between operations  0.65 us (1%)
    pallas_call x1, Pallas kernels, on_device(): pl.pallas_call(kernel, out_shape=(jax.ShapeDtypeStruct((4, 256), F32), ja...  39.9 us
    unnamed x8, local copies, waits for them, and re-layouts  3.89 us

profile of v1, /device:TPU:1, one launch (start us, length us, event | category | flops | bytes accessed | tf_op | source)
XLA Modules:
  0.0 44.5 jit_solution(12992464791981748186)
XLA Ops:
  0.6 0.0 copy-start
  0.6 1.2 %copy-done = f32[1024,256]{1,0:T(8,128)S(1)} copy-done((f32[1024,256]{1,0:T(8,128)S(1)}, f32[1024,256]{1,0:T(8,128)}, u32[]{:S(2)}) %copy-start) | copy-done | bytes 1048600
  1.9 0.0 copy-start.1
  1.9 0.7 %copy-done.1 = s32[1024]{0:T(1024)S(1)} copy-done((s32[1024]{0:T(1024)S(1)}, s32[1024]{0:T(1024)}, u32[]{:S(2)}) %copy-start.1) | copy-done | bytes 4120
  2.5 0.0 copy-start.2
  2.5 0.7 %copy-done.2 = s32[1024]{0:T(1024)S(1)} copy-done((s32[1024]{0:T(1024)S(1)}, s32[1024]{0:T(1024)}, u32[]{:S(2)}) %copy-start.2) | copy-done | bytes 4120
  3.2 39.9 %shard_map.50 = (f32[4,256]{1,0:T(4,128)S(1)}, f32[256,256]{1,0:T(8,128)S(1)}) custom-call(f32[1024,256]{1,0:T(8,128)S(1)} %copy-done, s32[1,1024]{1,0:T(1,128)S(1)} %bitcast.2, s32[1,1024]{1,0:T(1,128)S(1)} %bitcast.3), custom_call_target="tpu_custom_call" | custom-call | tf_op jit(solution)/shard_map/pallas_call | solution.py:174
  43.2 0.6 %copy.7 = f32[4,256]{1,0:T(4,128)} copy(f32[4,256]{1,0:T(4,128)S(1)} %get-tuple-element.4) | data formatting | bytes 8192
  43.8 0.7 %copy.8 = f32[256,256]{1,0:T(8,128)} copy(f32[256,256]{1,0:T(8,128)S(1)} %get-tuple-element.5) | data formatting | bytes 524288
Async XLA Ops:
  0.6 1.2 %copy-start = (f32[1024,256]{1,0:T(8,128)S(1)}, f32[1024,256]{1,0:T(8,128)}, u32[]{:S(2)}) copy-start(f32[1024,256]{1,0:T(8,128)} %design.1) | copy-start | bytes 3145732
  1.9 0.7 %copy-start.1 = (s32[1024]{0:T(1024)S(1)}, s32[1024]{0:T(1024)}, u32[]{:S(2)}) copy-start(s32[1024]{0:T(1024)} %param.4) | copy-start | bytes 12292
  2.5 0.7 %copy-start.2 = (s32[1024]{0:T(1024)S(1)}, s32[1024]{0:T(1024)}, u32[]{:S(2)}) copy-start(s32[1024]{0:T(1024)} %param.5) | copy-start | bytes 12292

commit v2 on v0

v2 whole, which is shorter than its diff:
```python
import functools

import jax
import jax.numpy as jnp
from jax import lax
from jax.experimental import pallas as pl
from jax.experimental.pallas import tpu as pltpu
from jax.sharding import PartitionSpec as P

MESH = pl.DeviceIdType.MESH
PARTS = 4
PART_ROWS = 64 // PARTS
PAIR, PLANE_SUM, LINE_SUM, ROUND, HALF = range(5)
PLANE = (
    (2, 2), (1, 2), (2, 1), (3, 2), (2, 3), (1, 1), (3, 3), (1, 3), (3, 1), (0, 2), (2, 0), (0, 1), (1, 0), (0, 3), (3, 0),
)
LINE = (4, 3, 5, 2, 6, 1, 7)
BF16, F32, I32 = jnp.bfloat16, jnp.float32, jnp.int32


def contract_rows(a, b):
    return lax.dot_general(a, b, (((0,), (0,)), ((), ())), preferred_element_type=F32)


def split(values):
    hi = values.astype(BF16)
    return hi, (values - hi.astype(F32)).astype(BF16)


def kernel(
    design, flips, ids, sketch_out, gram_out,
    rows_in, flips_in, ids_in, rows_hi, rows_lo, signs, mine, partner, from_partner, chip_sum, plane_in, line_in, gathered,
    load_sem, send_sem, recv_sem,
):
    wide, z = lax.axis_index("wide"), lax.axis_index("narrow")
    core, square = lax.rem(wide, 2), lax.div(wide, 2)
    x, y = lax.div(square, 4), lax.rem(square, 4)
    device = wide * 8 + z
    load_ids = pltpu.make_async_copy(ids, ids_in, load_sem.at[0])
    load_ids.start()
    load = pltpu.make_async_copy(design, rows_in, load_sem.at[1])
    load.start()
    load_flips = pltpu.make_async_copy(flips, flips_in, load_sem.at[2])
    load_flips.start()

    squares = [lax.rem(x + dx, 4) * 4 + lax.rem(y + dy, 4) for dx, dy in PLANE]
    plane = [(there * 2 + core, z) for there in squares]
    line = [(wide, lax.rem(z + dz, 8)) for dz in LINE]
    sibling = (wide + 1 - 2 * core, z)
    barrier = pltpu.get_barrier_semaphore()
    peers = plane + line + [sibling]
    for peer in peers:
        pl.semaphore_signal(barrier, inc=1, device_id=peer, device_id_type=MESH)

    def copy_of(step, a, source, target, peer):
        return pltpu.make_async_remote_copy(
            source, target, send_sem.at[step, a], recv_sem.at[step, a], device_id=peer, device_id_type=MESH
        )

    bit = lax.broadcasted_iota(I32, (32, 512), 0)
    lane = lax.broadcasted_iota(I32, (32, 512), 1)
    block, low = lax.shift_right_logical(lane, 7), lane & 127
    of_low = lax.shift_right_logical(low, jnp.minimum(bit, 7)) & 1
    of_device = lax.shift_right_logical(jnp.full((32, 512), device, I32), jnp.maximum(bit - 10, 0)) & 1
    of_device = jnp.where(bit >= 10, of_device, 0)
    first = jnp.where(bit < 7, of_low, of_device)
    masks = jnp.where(block == 0, first, jnp.where(bit == 6 + block, 1, 0)).astype(F32).astype(BF16)
    load_ids.wait()
    bit = lax.broadcasted_iota(I32, (32, 1024), 0)
    bits = (lax.shift_right_logical(jnp.broadcast_to(ids_in[...], (32, 1024)), bit) & 1).astype(F32).astype(BF16)
    counts = contract_rows(bits, masks)
    base = (1 - 2 * (counts[:, :128].astype(I32) & 1)).astype(F32)
    signs[0] = base.astype(BF16).reshape(16, PARTS, PART_ROWS, 128)
    for j in (1, 2, 3):
        signs[j] = (1.0 - 2.0 * counts[:, 128 * j : 128 * j + 128]).astype(BF16).reshape(16, PARTS, PART_ROWS, 128)

    load_flips.wait()
    flip = flips_in[...].astype(F32).astype(BF16)
    load.wait()
    hi, lo = split(rows_in[...] * (1.0 / 512.0))
    rows_hi[...] = hi
    rows_lo[...] = lo

    for a in range(PARTS):
        table = [signs[0, :, a].reshape(16 * PART_ROWS, 128)]
        for j in (1, 2, 3):
            other = signs[j, :, a].reshape(16 * PART_ROWS, 128)
            table = table + [s * other for s in table]
        table = [s * jnp.broadcast_to(flip[:, 128 * k : 128 * k + 128], (16 * PART_ROWS, 128)) for k, s in enumerate(table)]
        table = jnp.concatenate(table, axis=1)
        got = jnp.dot(table, rows_hi[...], preferred_element_type=F32)
        got = got + jnp.dot(table, rows_lo[...], preferred_element_type=F32)
        left, right = got[:, :128].reshape(16, PART_ROWS, 128), got[:, 128:].reshape(16, PART_ROWS, 128)
        mine[a] = jnp.where(core == 0, left, right)
        partner[a] = jnp.where(core == 0, right, left)
        if a == 0:
            pl.semaphore_wait(barrier, len(peers))
        copy_of(PAIR, a, partner.at[a], from_partner.at[a], sibling).start()

    def all_of(step, a):
        whole = (
            from_partner.at[a], plane_in.at[a], line_in.at[a, pl.ds(0, 7)],
            gathered.at[0, a, pl.ds(0, 15)], gathered.at[0, a],
        )[step]
        return copy_of(step, a, whole, whole, sibling)

    for a in range(PARTS):
        all_of(PAIR, a).wait_recv()
        chip_sum[a] = mine[a] + from_partner[a]
        for n in range(15):
            copy_of(PLANE_SUM, a, chip_sum.at[a, squares[n]], plane_in.at[a, n], plane[n]).start()
    for a in range(PARTS):
        all_of(PLANE_SUM, a).wait_recv()
        total = chip_sum[a, square]
        for n in range(15):
            total = total + plane_in[a, n]
        line_in[a, z] = total
        here = line_in.at[a, z]
        for n in range(7):
            copy_of(LINE_SUM, a, here, here, line[n]).start()
    for a in range(PARTS):
        all_of(LINE_SUM, a).wait_recv()
        total = line_in[a, 0]
        for k in range(1, 8):
            total = total + line_in[a, k]
        gathered[core, a, square] = total
        here = gathered.at[core, a, square]
        for n in range(15):
            copy_of(ROUND, a, here, here, plane[n]).start()
    for a in range(PARTS):
        all_of(ROUND, a).wait_recv()
        here = gathered.at[core, a]
        copy_of(HALF, a, here, here, sibling).start()
    gram = None
    for a in range(PARTS):
        all_of(HALF, a).wait_recv()
        left, right = gathered[0, a].reshape(16 * PART_ROWS, 128), gathered[1, a].reshape(16 * PART_ROWS, 128)
        hi, lo = split(jnp.concatenate([left, right], axis=1))
        cross = contract_rows(hi, lo)
        term = contract_rows(hi, hi) + (cross + cross.T)
        gram = term if gram is None else gram + term
    gram_out[...] = gram * (1.0 / 1024.0)
    row = core * 32 + z * 4
    part, row = lax.div(row, PART_ROWS), lax.rem(row, PART_ROWS)
    tile = pl.ds(pl.multiple_of(lax.div(row, 8) * 8, 8), 8)
    for h in range(2):
        eight = gathered[h, part, square, tile]
        sketch_out[:, 128 * h : 128 * h + 128] = jnp.where(lax.rem(z, 2) == 0, eight[:4], eight[4:])
    for step in range(5):
        for a in range(PARTS):
            all_of(step, a).wait_send()


def on_device(design, sign_flips, sample_ids):
    dma = pltpu.SemaphoreType.DMA
    vmem, hbm = pl.BlockSpec(memory_space=pltpu.VMEM), pl.BlockSpec(memory_space=pltpu.HBM)
    return pl.pallas_call(
        kernel,
        out_shape=(jax.ShapeDtypeStruct((4, 256), F32), jax.ShapeDtypeStruct((256, 256), F32)),
        in_specs=[hbm, hbm, hbm],
        out_specs=(vmem, vmem),
        scratch_shapes=[
            pltpu.VMEM((1024, 256), F32),
            pltpu.VMEM((1, 1024), I32),
            pltpu.VMEM((1, 1024), I32),
            pltpu.VMEM((1024, 256), BF16),
            pltpu.VMEM((1024, 256), BF16),
            pltpu.VMEM((4, 16, PARTS, PART_ROWS, 128), BF16),
            pltpu.VMEM((PARTS, 16, PART_ROWS, 128), F32),
            pltpu.VMEM((PARTS, 16, PART_ROWS, 128), F32),
            pltpu.VMEM((PARTS, 16, PART_ROWS, 128), F32),
            pltpu.VMEM((PARTS, 16, PART_ROWS, 128), F32),
            pltpu.VMEM((PARTS, 15, PART_ROWS, 128), F32),
            pltpu.VMEM((PARTS, 8, PART_ROWS, 128), F32),
            pltpu.VMEM((2, PARTS, 16, PART_ROWS, 128), F32),
            dma((3,)), dma((5, PARTS)), dma((5, PARTS)),
        ],
        compiler_params=pltpu.CompilerParams(collective_id=0, has_side_effects=True, vmem_limit_bytes=40 << 20),
    )(*[pltpu.with_memory_space_constraint(v, pltpu.HBM) for v in (design, sign_flips.reshape(1, 1024), sample_ids.reshape(1, 1024))])


def solution(mesh):
    placed = (P(("wide", "narrow"), None), P(("wide", "narrow")), P())
    return jax.shard_map(
        on_device,
        mesh=mesh,
        in_specs=placed,
        out_specs=(P(("wide", "narrow"), None), P()),
        check_vma=False,
    )
```

time: 766 us -> 35.1 us (0.05)
  waiting for transfers between devices: 711 us -> 0 us
  Pallas kernels: 0 us -> 33.1 us
  starting transfers between devices: 23.4 us -> 0 us
  between operations: 14.1 us -> 0.64 us
    unnamed x3 -> x0, waiting for transfers between devices: 256 us -> none
    psum x1 -> x0, waiting for transfers between devices: 254 us -> none  [on_device(): gram_matrix = lax.psum(own_term, ('wide', 'narrow')) / samples_all]
    ppermute x8 -> x0, waiting for transfers between devices: 201 us -> none  [swapped(): lax.ppermute(x, axis, [(i, i ^ 1 << distance) for i in range(lax.axis_siz...]
    pallas_call x0 -> x1, Pallas kernels: none -> 33.1 us  [on_device(): pl.pallas_call(kernel, out_shape=(jax.ShapeDtypeStruct((4, 256), F32), ja...]
    ppermute x8 -> x0, starting transfers between devices: 23.3 us -> none  [swapped(): lax.ppermute(x, axis, [(i, i ^ 1 << distance) for i in range(lax.axis_siz...]
  transfers between devices with their start and end apart: 10 -> 0, of which waited for: 10 -> 0; matrix products, arithmetic and copies ran while one was open for 0% -> 0% of each run, Pallas kernels for 0% -> 0%
where the time goes in v2:
time: 35.1 us; the launch traced here: 35 us
  Pallas kernels  33.1 us (94%)
  local copies, waits for them, and re-layouts  1.3 us (4%)
  between operations  0.64 us (2%)
    pallas_call x1, Pallas kernels, on_device(): pl.pallas_call(kernel, out_shape=(jax.ShapeDtypeStruct((4, 256), F32), ja...  33.1 us
    unnamed x2, local copies, waits for them, and re-layouts  1.3 us

profile of v2, /device:TPU:1, one launch (start us, length us, event | category | flops | bytes accessed | tf_op | source)
XLA Modules:
  0.0 35.0 jit_solution(8148137785356896613)
XLA Ops:
  0.6 33.1 %shard_map.50 = (f32[4,256]{1,0:T(4,128)S(1)}, f32[256,256]{1,0:T(8,128)S(1)}) custom-call(f32[1024,256]{1,0:T(8,128)} %design.1, s32[1,1024]{1,0:T(1,128)} %bitcast.2, s32[1,1024]{1,0:T(1,128)} %bitcast.3), custom_call_target="tpu_custom_call" | custom-call | tf_op jit(solution)/shard_map/pallas_call | solution.py:157
  33.7 0.6 %copy.7 = f32[4,256]{1,0:T(4,128)} copy(f32[4,256]{1,0:T(4,128)S(1)} %get-tuple-element.4) | data formatting | bytes 8192
  34.3 0.7 %copy.8 = f32[256,256]{1,0:T(8,128)} copy(f32[256,256]{1,0:T(8,128)S(1)} %get-tuple-element.5) | data formatting | bytes 524288

commit v3 on v2

v3 whole, which is shorter than its diff:
```python
import functools

import jax
import jax.numpy as jnp
from jax import lax
from jax.experimental import pallas as pl
from jax.experimental.pallas import tpu as pltpu
from jax.sharding import PartitionSpec as P

MESH = pl.DeviceIdType.MESH
PARTS, LEVEL_PART = 4, 1
SQUARE_ROWS, LEVEL_ROWS = 16, 32
SQUARE_PARTS = [a for a in range(PARTS) if a != LEVEL_PART]
PAIR, SUM, ACROSS, ROUND, HALF = range(5)
PLANE = (
    (2, 2), (1, 2), (2, 1), (3, 2), (2, 3), (1, 1), (3, 3), (1, 3), (3, 1), (0, 2), (2, 0), (0, 1), (1, 0), (0, 3), (3, 0),
)
LINE = (4, 3, 5, 2, 6, 1, 7)
BF16, F32, I32 = jnp.bfloat16, jnp.float32, jnp.int32


def contract_rows(a, b):
    return lax.dot_general(a, b, (((0,), (0,)), ((), ())), preferred_element_type=F32)


def split(values):
    hi = values.astype(BF16)
    return hi, (values - hi.astype(F32)).astype(BF16)


def kernel(
    design, flips, ids, sketch_out, gram_out,
    rows_in, flips_in, ids_in, rows_hi, rows_lo, square_signs, level_signs, mine, partner, from_partner, chip_sum,
    plane_in, line_across, line_in, plane_across, gathered,
    load_sem, send_sem, recv_sem,
):
    wide, z = lax.axis_index("wide"), lax.axis_index("narrow")
    core, square = lax.rem(wide, 2), lax.div(wide, 2)
    x, y = lax.div(square, 4), lax.rem(square, 4)
    device = wide * 8 + z
    load_ids = pltpu.make_async_copy(ids, ids_in, load_sem.at[0])
    load_ids.start()
    load = pltpu.make_async_copy(design, rows_in, load_sem.at[1])
    load.start()
    load_flips = pltpu.make_async_copy(flips, flips_in, load_sem.at[2])
    load_flips.start()

    squares = [lax.rem(x + dx, 4) * 4 + lax.rem(y + dy, 4) for dx, dy in PLANE]
    plane = [(there * 2 + core, z) for there in squares]
    levels = [lax.rem(z + dz, 8) for dz in LINE]
    line = [(wide, there) for there in levels]
    sibling = (wide + 1 - 2 * core, z)
    barrier = pltpu.get_barrier_semaphore()
    peers = plane + line + [sibling]
    for peer in peers:
        pl.semaphore_signal(barrier, inc=1, device_id=peer, device_id_type=MESH)

    def copy_of(step, a, source, target, peer):
        return pltpu.make_async_remote_copy(
            source, target, send_sem.at[step, a], recv_sem.at[step, a], device_id=peer, device_id_type=MESH
        )

    bit = lax.broadcasted_iota(I32, (32, 512), 0)
    lane = lax.broadcasted_iota(I32, (32, 512), 1)
    block, low = lax.shift_right_logical(lane, 7), lane & 127
    of_low = lax.shift_right_logical(low, jnp.minimum(bit, 7)) & 1
    of_device = lax.shift_right_logical(jnp.full((32, 512), device, I32), jnp.maximum(bit - 10, 0)) & 1
    of_device = jnp.where(bit >= 10, of_device, 0)
    first = jnp.where(bit < 7, of_low, of_device)
    masks = jnp.where(block == 0, first, jnp.where(bit == 6 + block, 1, 0)).astype(F32).astype(BF16)
    load_ids.wait()
    bit = lax.broadcasted_iota(I32, (32, 1024), 0)
    bits = (lax.shift_right_logical(jnp.broadcast_to(ids_in[...], (32, 1024)), bit) & 1).astype(F32).astype(BF16)
    counts = contract_rows(bits, masks)
    base = (1 - 2 * (counts[:, :128].astype(I32) & 1)).astype(F32)
    for j in range(4):
        sign = (base if j == 0 else 1.0 - 2.0 * counts[:, 128 * j : 128 * j + 128]).astype(BF16)
        square_signs[j] = sign[:768].reshape(16, 3, SQUARE_ROWS, 128)
        level_signs[j] = sign[768:]

    load_flips.wait()
    flip = flips_in[...].astype(F32).astype(BF16)
    load.wait()
    hi, lo = split(rows_in[...] * (1.0 / 512.0))
    rows_hi[...] = hi
    rows_lo[...] = lo

    def signs_of(a, j):
        if a == LEVEL_PART:
            return level_signs[j]
        return square_signs[j, :, SQUARE_PARTS.index(a)].reshape(256, 128)

    for a in range(PARTS):
        table = [signs_of(a, 0)]
        for j in (1, 2, 3):
            other = signs_of(a, j)
            table = table + [s * other for s in table]
        table = [s * jnp.broadcast_to(flip[:, 128 * k : 128 * k + 128], (256, 128)) for k, s in enumerate(table)]
        table = jnp.concatenate(table, axis=1)
        got = jnp.dot(table, rows_hi[...], preferred_element_type=F32)
        got = got + jnp.dot(table, rows_lo[...], preferred_element_type=F32)
        left, right = got[:, :128], got[:, 128:]
        mine[a] = jnp.where(core == 0, left, right)
        partner[a] = jnp.where(core == 0, right, left)
    pl.semaphore_wait(barrier, len(peers))
    for a in range(PARTS):
        copy_of(PAIR, a, partner.at[a], from_partner.at[a], sibling).start()

    def of_square(there):
        return pl.ds(pl.multiple_of(there * SQUARE_ROWS, 8), SQUARE_ROWS)

    def of_level(there):
        return pl.ds(pl.multiple_of(there * LEVEL_ROWS, 8), LEVEL_ROWS)

    def all_of(step, a):
        if step == PAIR:
            whole = from_partner.at[a]
        elif step == HALF:
            whole = gathered.at[0, a]
        elif a == LEVEL_PART:
            whole = (line_in, plane_across.at[pl.ds(0, 15)], gathered.at[0, a, pl.ds(0, 7 * LEVEL_ROWS)])[step - SUM]
        else:
            b = SQUARE_PARTS.index(a)
            whole = (
                plane_in.at[b], line_across.at[b, pl.ds(0, 7)], gathered.at[0, a, pl.ds(0, 15 * SQUARE_ROWS)]
            )[step - SUM]
        return copy_of(step, a, whole, whole, sibling)

    for a in range(PARTS):
        all_of(PAIR, a).wait_recv()
        chip_sum[a] = mine[a] + from_partner[a]
        if a == LEVEL_PART:
            for n in range(7):
                copy_of(SUM, a, chip_sum.at[a, of_level(levels[n])], line_in.at[n], line[n]).start()
        else:
            b = SQUARE_PARTS.index(a)
            for n in range(15):
                copy_of(SUM, a, chip_sum.at[a, of_square(squares[n])], plane_in.at[b, n], plane[n]).start()
    for a in range(PARTS):
        all_of(SUM, a).wait_recv()
        if a == LEVEL_PART:
            total = chip_sum[a, of_level(z)]
            for n in range(7):
                total = total + line_in[n]
            plane_across[square] = total
            here = plane_across.at[square]
            for n in range(15):
                copy_of(ACROSS, a, here, here, plane[n]).start()
        else:
            b = SQUARE_PARTS.index(a)
            total = chip_sum[a, of_square(square)]
            for n in range(15):
                total = total + plane_in[b, n]
            line_across[b, z] = total
            here = line_across.at[b, z]
            for n in range(7):
                copy_of(ACROSS, a, here, here, line[n]).start()
    for a in range(PARTS):
        all_of(ACROSS, a).wait_recv()
        if a == LEVEL_PART:
            terms, own, others = [plane_across[k] for k in range(16)], of_level(z), line
        else:
            b = SQUARE_PARTS.index(a)
            terms, own, others = [line_across[b, k] for k in range(8)], of_square(square), plane
        total = terms[0]
        for term in terms[1:]:
            total = total + term
        gathered[core, a, own] = total
        here = gathered.at[core, a, own]
        for peer in others:
            copy_of(ROUND, a, here, here, peer).start()
    for a in range(PARTS):
        all_of(ROUND, a).wait_recv()
        here = gathered.at[core, a]
        copy_of(HALF, a, here, here, sibling).start()
    gram = None
    for a in range(PARTS):
        all_of(HALF, a).wait_recv()
        left, right = gathered[0, a], gathered[1, a]
        hi, lo = split(jnp.concatenate([left, right], axis=1))
        cross = contract_rows(hi, lo)
        term = contract_rows(hi, hi) + (cross + cross.T)
        gram = term if gram is None else gram + term
    gram_out[...] = gram * (1.0 / 1024.0)
    row = device * 4
    b = lax.div(lax.rem(row, 48), 16)
    in_square = lax.div(row, 48) * SQUARE_ROWS + lax.rem(row, 16)
    part = jnp.where(row < 768, jnp.where(b >= LEVEL_PART, b + 1, b), LEVEL_PART)
    tile = pl.ds(pl.multiple_of(lax.div(jnp.where(row < 768, in_square, row - 768), 8) * 8, 8), 8)
    for h in range(2):
        eight = gathered[h, part, tile]
        sketch_out[:, 128 * h : 128 * h + 128] = jnp.where(lax.rem(z, 2) == 0, eight[:4], eight[4:])
    for step in range(5):
        for a in range(PARTS):
            all_of(step, a).wait_send()


def on_device(design, sign_flips, sample_ids):
    dma = pltpu.SemaphoreType.DMA
    vmem, hbm = pl.BlockSpec(memory_space=pltpu.VMEM), pl.BlockSpec(memory_space=pltpu.HBM)
    sketch, gram = pl.pallas_call(
        kernel,
        out_shape=(pltpu.VMEM((4, 256), F32), pltpu.VMEM((256, 256), F32)),
        in_specs=[hbm, hbm, hbm],
        out_specs=(vmem, vmem),
        scratch_shapes=[
            pltpu.VMEM((1024, 256), F32),
            pltpu.VMEM((1, 1024), I32),
            pltpu.VMEM((1, 1024), I32),
            pltpu.VMEM((1024, 256), BF16),
            pltpu.VMEM((1024, 256), BF16),
            pltpu.VMEM((4, 16, 3, SQUARE_ROWS, 128), BF16),
            pltpu.VMEM((4, 256, 128), BF16),
            pltpu.VMEM((PARTS, 256, 128), F32),
            pltpu.VMEM((PARTS, 256, 128), F32),
            pltpu.VMEM((PARTS, 256, 128), F32),
            pltpu.VMEM((PARTS, 256, 128), F32),
            pltpu.VMEM((3, 15, SQUARE_ROWS, 128), F32),
            pltpu.VMEM((3, 8, SQUARE_ROWS, 128), F32),
            pltpu.VMEM((7, LEVEL_ROWS, 128), F32),
            pltpu.VMEM((16, LEVEL_ROWS, 128), F32),
            pltpu.VMEM((2, PARTS, 256, 128), F32),
            dma((3,)), dma((5, PARTS)), dma((5, PARTS)),
        ],
        compiler_params=pltpu.CompilerParams(collective_id=0, has_side_effects=True, vmem_limit_bytes=40 << 20),
    )(*[pltpu.with_memory_space_constraint(v, pltpu.HBM) for v in (design, sign_flips.reshape(1, 1024), sample_ids.reshape(1, 1024))])
    return pl.pallas_call(
        hand_out,
        out_shape=(jax.ShapeDtypeStruct((4, 256), F32), jax.ShapeDtypeStruct((256, 256), F32)),
        in_specs=[vmem, vmem],
        out_specs=(hbm, hbm),
        scratch_shapes=[dma((2,))],
    )(pltpu.with_memory_space_constraint(sketch, pltpu.VMEM), pltpu.with_memory_space_constraint(gram, pltpu.VMEM))


def hand_out(sketch, gram, sketch_out, gram_out, sem):
    first = pltpu.make_async_copy(gram, gram_out, sem.at[0])
    second = pltpu.make_async_copy(sketch, sketch_out, sem.at[1])
    first.start()
    second.start()
    first.wait()
    second.wait()


def solution(mesh):
    placed = (P(("wide", "narrow"), None), P(("wide", "narrow")), P())
    return jax.shard_map(
        on_device,
        mesh=mesh,
        in_specs=placed,
        out_specs=(P(("wide", "narrow"), None), P()),
        check_vma=False,
    )
```

time: 35.1 us -> 32.7 us (0.932)
  local copies, waits for them, and re-layouts: 1.3 us -> 0 us
  Pallas kernels: 33.1 us -> 31.9 us
    unnamed x2 -> x0, local copies, waits for them, and re-layouts: 1.3 us -> none
    pallas_call x1 -> x2, Pallas kernels: 33.1 us -> 31.9 us  [the longest x1 31.2 us: on_device(): pl.pallas_call(kernel, out_shape=(pltpu.VMEM((4, 256), F32), pltpu.VMEM((...]
where the time goes in v3:
time: 32.7 us; the launch traced here: 32.6 us
  Pallas kernels  31.9 us (98%)
  between operations  0.64 us (2%)
    pallas_call x1, Pallas kernels, on_device(): pl.pallas_call(kernel, out_shape=(pltpu.VMEM((4, 256), F32), pltpu.VMEM((...  31.2 us
    pallas_call x1, Pallas kernels, on_device(): pl.pallas_call(hand_out, out_shape=(jax.ShapeDtypeStruct((4, 256), F32),...  0.72 us

profile of v3, /device:TPU:1, one launch (start us, length us, event | category | flops | bytes accessed | tf_op | source)
XLA Modules:
  0.0 32.6 jit_solution(4598592287478013692)
XLA Ops:
  0.6 31.2 %shard_map.50 = (f32[4,256]{1,0:T(4,128)S(1)}, f32[256,256]{1,0:T(8,128)S(1)}) custom-call(f32[1024,256]{1,0:T(8,128)} %design.1, s32[1,1024]{1,0:T(1,128)} %bitcast.2, s32[1,1024]{1,0:T(1,128)} %bitcast.3), custom_call_target="tpu_custom_call" | custom-call | tf_op jit(solution)/shard_map/pallas_call | solution.py:201
  31.9 0.7 %shard_map.51 = (f32[4,256]{1,0:T(4,128)}, f32[256,256]{1,0:T(8,128)}) custom-call(f32[4,256]{1,0:T(4,128)S(1)} %get-tuple-element.4.sketch, f32[256,256]{1,0:T(8,128)S(1)} %get-tuple-element.5.gram), custom_call_target="tpu_custom_call" | custom-call | tf_op jit(solution)/shard_map/pallas_call | solution.py:227

commit v4 on v3

--- a/solution.py
+++ b/solution.py
@@ -11,10 +11,12 @@
 PARTS, LEVEL_PART = 4, 1
 SQUARE_ROWS, LEVEL_ROWS = 16, 32
 SQUARE_PARTS = [a for a in range(PARTS) if a != LEVEL_PART]
+ORDER = tuple((stage, a) for stage in range(3) for a in range(PARTS))
 PAIR, SUM, ACROSS, ROUND, HALF = range(5)
 PLANE = (
     (2, 2), (1, 2), (2, 1), (3, 2), (2, 3), (1, 1), (3, 3), (1, 3), (3, 1), (0, 2), (2, 0), (0, 1), (1, 0), (0, 3), (3, 0),
 )
+BY_START = tuple(sorted(range(16), key=lambda q: (min(q // 4, 4 - q // 4) + min(q % 4, 4 - q % 4), q)))
 LINE = (4, 3, 5, 2, 6, 1, 7)
 BF16, F32, I32 = jnp.bfloat16, jnp.float32, jnp.int32
 
@@ -30,7 +32,7 @@
 
 def kernel(
     design, flips, ids, sketch_out, gram_out,
-    rows_in, flips_in, ids_in, rows_hi, rows_lo, square_signs, level_signs, mine, partner, from_partner, chip_sum,
+    rows_in, flips_in, ids_in, rows_hi, rows_lo, square_signs, level_signs, mine, partner, from_partner, all_sums,
     plane_in, line_across, line_in, plane_across, gathered,
     load_sem, send_sem, recv_sem,
 ):
@@ -50,6 +52,10 @@
     levels = [lax.rem(z + dz, 8) for dz in LINE]
     line = [(wide, there) for there in levels]
     sibling = (wide + 1 - 2 * core, z)
+    rank = sum(jnp.where(square == there, p, 0) for p, there in enumerate(BY_START))
+    early_squares = [jnp.where(k < rank, BY_START[k], BY_START[k + 1]) for k in range(15)]
+    early_plane = [(there * 2 + core, z) for there in early_squares]
+    early_line = [(wide, jnp.where(k < z, k, k + 1)) for k in range(7)]
     barrier = pltpu.get_barrier_semaphore()
     peers = plane + line + [sibling]
     for peer in peers:
@@ -57,7 +63,7 @@
 
     def copy_of(step, a, source, target, peer):
         return pltpu.make_async_remote_copy(
-            source, target, send_sem.at[step, a], recv_sem.at[step, a], device_id=peer, device_id_type=MESH
+            source, target, send_sem.at[step], recv_sem.at[step, a], device_id=peer, device_id_type=MESH
         )
 
     bit = lax.broadcasted_iota(I32, (32, 512), 0)
@@ -106,11 +112,11 @@
     for a in range(PARTS):
         copy_of(PAIR, a, partner.at[a], from_partner.at[a], sibling).start()
 
-    def of_square(there):
-        return pl.ds(pl.multiple_of(there * SQUARE_ROWS, 8), SQUARE_ROWS)
-
-    def of_level(there):
-        return pl.ds(pl.multiple_of(there * LEVEL_ROWS, 8), LEVEL_ROWS)
+    def of_square(there, first=0):
+        return pl.ds(pl.multiple_of(first + there * SQUARE_ROWS, 8), SQUARE_ROWS)
+
+    def of_level(there, first=0):
+        return pl.ds(pl.multiple_of(first + there * LEVEL_ROWS, 8), LEVEL_ROWS)
 
     def all_of(step, a):
         if step == PAIR:
@@ -128,18 +134,18 @@
 
     for a in range(PARTS):
         all_of(PAIR, a).wait_recv()
-        chip_sum[a] = mine[a] + from_partner[a]
+        all_sums[pl.ds(256 * a, 256)] = mine[a] + from_partner[a]
         if a == LEVEL_PART:
             for n in range(7):
-                copy_of(SUM, a, chip_sum.at[a, of_level(levels[n])], line_in.at[n], line[n]).start()
+                copy_of(SUM, a, all_sums.at[of_level(levels[n], 256 * a)], line_in.at[n], line[n]).start()
         else:
             b = SQUARE_PARTS.index(a)
             for n in range(15):
-                copy_of(SUM, a, chip_sum.at[a, of_square(squares[n])], plane_in.at[b, n], plane[n]).start()
-    for a in range(PARTS):
+                copy_of(SUM, a, all_sums.at[of_square(squares[n], 256 * a)], plane_in.at[b, n], plane[n]).start()
+    def add_up(a):
         all_of(SUM, a).wait_recv()
         if a == LEVEL_PART:
-            total = chip_sum[a, of_level(z)]
+            total = all_sums[of_level(z, 256 * a)]
             for n in range(7):
                 total = total + line_in[n]
             plane_across[square] = total
@@ -148,20 +154,21 @@
                 copy_of(ACROSS, a, here, here, plane[n]).start()
         else:
             b = SQUARE_PARTS.index(a)
-            total = chip_sum[a, of_square(square)]
+            total = all_sums[of_square(square, 256 * a)]
             for n in range(15):
                 total = total + plane_in[b, n]
             line_across[b, z] = total
             here = line_across.at[b, z]
             for n in range(7):
-                copy_of(ACROSS, a, here, here, line[n]).start()
-    for a in range(PARTS):
+                copy_of(ACROSS, a, here, here, early_line[n]).start()
+
+    def add_across(a):
         all_of(ACROSS, a).wait_recv()
         if a == LEVEL_PART:
-            terms, own, others = [plane_across[k] for k in range(16)], of_level(z), line
-        else:
-            b = SQUARE_PARTS.index(a)
-            terms, own, others = [line_across[b, k] for k in range(8)], of_square(square), plane
+            terms, own, others = [plane_across[k] for k in range(16)], of_level(z), early_line
+        else:
+            b = SQUARE_PARTS.index(a)
+            terms, own, others = [line_across[b, k] for k in range(8)], of_square(square), early_plane
         total = terms[0]
         for term in terms[1:]:
             total = total + term
@@ -169,10 +176,14 @@
         here = gathered.at[core, a, own]
         for peer in others:
             copy_of(ROUND, a, here, here, peer).start()
-    for a in range(PARTS):
+
+    def pass_on(a):
         all_of(ROUND, a).wait_recv()
         here = gathered.at[core, a]
         copy_of(HALF, a, here, here, sibling).start()
+
+    for stage, a in ORDER:
+        (add_up, add_across, pass_on)[stage](a)
     gram = None
     for a in range(PARTS):
         all_of(HALF, a).wait_recv()
@@ -190,9 +201,9 @@
     for h in range(2):
         eight = gathered[h, part, tile]
         sketch_out[:, 128 * h : 128 * h + 128] = jnp.where(lax.rem(z, 2) == 0, eight[:4], eight[4:])
-    for step in range(5):
-        for a in range(PARTS):
-            all_of(step, a).wait_send()
+    for step, rows in enumerate((1024, 944, 816, 944, 1024)):
+        whole = all_sums.at[pl.ds(0, rows)]
+        copy_of(step, 0, whole, whole, sibling).wait_send()
 
 
 def on_device(design, sign_flips, sample_ids):
@@ -214,13 +225,13 @@
             pltpu.VMEM((PARTS, 256, 128), F32),
             pltpu.VMEM((PARTS, 256, 128), F32),
             pltpu.VMEM((PARTS, 256, 128), F32),
-            pltpu.VMEM((PARTS, 256, 128), F32),
+            pltpu.VMEM((1024, 128), F32),
             pltpu.VMEM((3, 15, SQUARE_ROWS, 128), F32),
             pltpu.VMEM((3, 8, SQUARE_ROWS, 128), F32),
             pltpu.VMEM((7, LEVEL_ROWS, 128), F32),
             pltpu.VMEM((16, LEVEL_ROWS, 128), F32),
             pltpu.VMEM((2, PARTS, 256, 128), F32),
-            dma((3,)), dma((5, PARTS)), dma((5, PARTS)),
+            dma((3,)), dma((5,)), dma((5, PARTS)),
         ],
         compiler_params=pltpu.CompilerParams(collective_id=0, has_side_effects=True, vmem_limit_bytes=40 << 20),
     )(*[pltpu.with_memory_space_constraint(v, pltpu.HBM) for v in (design, sign_flips.reshape(1, 1024), sample_ids.reshape(1, 1024))])

time: 32.7 us -> 32.5 us (level)
  no operation moved by 1% of the time
where the time goes in v4:
time: 32.5 us; the launch traced here: 32.4 us
  Pallas kernels  31.7 us (98%)
  between operations  0.64 us (2%)
    pallas_call x1, Pallas kernels, on_device(): pl.pallas_call(kernel, out_shape=(pltpu.VMEM((4, 256), F32), pltpu.VMEM((...  31 us
    pallas_call x1, Pallas kernels, on_device(): pl.pallas_call(hand_out, out_shape=(jax.ShapeDtypeStruct((4, 256), F32),...  0.72 us

profile of v4, /device:TPU:1, one launch (start us, length us, event | category | flops | bytes accessed | tf_op | source)
XLA Modules:
  0.0 32.4 jit_solution(7668951039785446194)
XLA Ops:
  0.6 31.0 %shard_map.50 = (f32[4,256]{1,0:T(4,128)S(1)}, f32[256,256]{1,0:T(8,128)S(1)}) custom-call(f32[1024,256]{1,0:T(8,128)} %design.1, s32[1,1024]{1,0:T(1,128)} %bitcast.2, s32[1,1024]{1,0:T(1,128)} %bitcast.3), custom_call_target="tpu_custom_call" | custom-call | tf_op jit(solution)/shard_map/pallas_call | solution.py:212
  31.7 0.7 %shard_map.51 = (f32[4,256]{1,0:T(4,128)}, f32[256,256]{1,0:T(8,128)}) custom-call(f32[4,256]{1,0:T(4,128)S(1)} %get-tuple-element.4.sketch, f32[256,256]{1,0:T(8,128)S(1)} %get-tuple-element.5.gram), custom_call_target="tpu_custom_call" | custom-call | tf_op jit(solution)/shard_map/pallas_call | solution.py:238

commit v5 on v4

--- a/solution.py
+++ b/solution.py
@@ -8,9 +8,11 @@
 from jax.sharding import PartitionSpec as P
 
 MESH = pl.DeviceIdType.MESH
-PARTS, LEVEL_PART = 4, 1
-SQUARE_ROWS, LEVEL_ROWS = 16, 32
-SQUARE_PARTS = [a for a in range(PARTS) if a != LEVEL_PART]
+PARTS, LEVEL_PARTS = 5, [1, 3]
+SQUARE_ROWS, LEVEL_ROWS = 16, 16
+SQUARE_PARTS = [a for a in range(PARTS) if a not in LEVEL_PARTS]
+SIZES = [128 if a in LEVEL_PARTS else 256 for a in range(PARTS)]
+STARTS = [sum(SIZES[:a]) for a in range(PARTS)]
 ORDER = tuple((stage, a) for stage in range(3) for a in range(PARTS))
 PAIR, SUM, ACROSS, ROUND, HALF = range(5)
 PLANE = (
@@ -82,7 +84,7 @@
     for j in range(4):
         sign = (base if j == 0 else 1.0 - 2.0 * counts[:, 128 * j : 128 * j + 128]).astype(BF16)
         square_signs[j] = sign[:768].reshape(16, 3, SQUARE_ROWS, 128)
-        level_signs[j] = sign[768:]
+        level_signs[j] = sign[768:].reshape(2, 128, 128)
 
     load_flips.wait()
     flip = flips_in[...].astype(F32).astype(BF16)
@@ -92,8 +94,8 @@
     rows_lo[...] = lo
 
     def signs_of(a, j):
-        if a == LEVEL_PART:
-            return level_signs[j]
+        if a in LEVEL_PARTS:
+            return level_signs[j, LEVEL_PARTS.index(a)]
         return square_signs[j, :, SQUARE_PARTS.index(a)].reshape(256, 128)
 
     for a in range(PARTS):
@@ -101,16 +103,17 @@
         for j in (1, 2, 3):
             other = signs_of(a, j)
             table = table + [s * other for s in table]
-        table = [s * jnp.broadcast_to(flip[:, 128 * k : 128 * k + 128], (256, 128)) for k, s in enumerate(table)]
+        table = [s * jnp.broadcast_to(flip[:, 128 * k : 128 * k + 128], (SIZES[a], 128)) for k, s in enumerate(table)]
         table = jnp.concatenate(table, axis=1)
         got = jnp.dot(table, rows_hi[...], preferred_element_type=F32)
         got = got + jnp.dot(table, rows_lo[...], preferred_element_type=F32)
         left, right = got[:, :128], got[:, 128:]
-        mine[a] = jnp.where(core == 0, left, right)
-        partner[a] = jnp.where(core == 0, right, left)
+        mine[a, : SIZES[a]] = jnp.where(core == 0, left, right)
+        partner[a, : SIZES[a]] = jnp.where(core == 0, right, left)
     pl.semaphore_wait(barrier, len(peers))
     for a in range(PARTS):
-        copy_of(PAIR, a, partner.at[a], from_partner.at[a], sibling).start()
+        rows = pl.ds(0, SIZES[a])
+        copy_of(PAIR, a, partner.at[a, rows], from_partner.at[a, rows], sibling).start()
 
     def of_square(there, first=0):
         return pl.ds(pl.multiple_of(first + there * SQUARE_ROWS, 8), SQUARE_ROWS)
@@ -120,11 +123,12 @@
 
     def all_of(step, a):
         if step == PAIR:
-            whole = from_partner.at[a]
+            whole = from_partner.at[a, pl.ds(0, SIZES[a])]
         elif step == HALF:
-            whole = gathered.at[0, a]
-        elif a == LEVEL_PART:
-            whole = (line_in, plane_across.at[pl.ds(0, 15)], gathered.at[0, a, pl.ds(0, 7 * LEVEL_ROWS)])[step - SUM]
+            whole = gathered.at[0, a, pl.ds(0, SIZES[a])]
+        elif a in LEVEL_PARTS:
+            b = LEVEL_PARTS.index(a)
+            whole = (line_in.at[b], plane_across.at[b, pl.ds(0, 15)], gathered.at[0, a, pl.ds(0, 7 * LEVEL_ROWS)])[step - SUM]
         else:
             b = SQUARE_PARTS.index(a)
             whole = (
@@ -134,27 +138,29 @@
 
     for a in range(PARTS):
         all_of(PAIR, a).wait_recv()
-        all_sums[pl.ds(256 * a, 256)] = mine[a] + from_partner[a]
-        if a == LEVEL_PART:
+        all_sums[pl.ds(STARTS[a], SIZES[a])] = mine[a, : SIZES[a]] + from_partner[a, : SIZES[a]]
+        if a in LEVEL_PARTS:
+            b = LEVEL_PARTS.index(a)
             for n in range(7):
-                copy_of(SUM, a, all_sums.at[of_level(levels[n], 256 * a)], line_in.at[n], line[n]).start()
+                copy_of(SUM, a, all_sums.at[of_level(levels[n], STARTS[a])], line_in.at[b, n], line[n]).start()
         else:
             b = SQUARE_PARTS.index(a)
             for n in range(15):
-                copy_of(SUM, a, all_sums.at[of_square(squares[n], 256 * a)], plane_in.at[b, n], plane[n]).start()
+                copy_of(SUM, a, all_sums.at[of_square(squares[n], STARTS[a])], plane_in.at[b, n], plane[n]).start()
     def add_up(a):
         all_of(SUM, a).wait_recv()
-        if a == LEVEL_PART:
-            total = all_sums[of_level(z, 256 * a)]
+        if a in LEVEL_PARTS:
+            b = LEVEL_PARTS.index(a)
+            total = all_sums[of_level(z, STARTS[a])]
             for n in range(7):
-                total = total + line_in[n]
-            plane_across[square] = total
-            here = plane_across.at[square]
+                total = total + line_in[b, n]
+            plane_across[b, square] = total
+            here = plane_across.at[b, square]
             for n in range(15):
                 copy_of(ACROSS, a, here, here, plane[n]).start()
         else:
             b = SQUARE_PARTS.index(a)
-            total = all_sums[of_square(square, 256 * a)]
+            total = all_sums[of_square(square, STARTS[a])]
             for n in range(15):
                 total = total + plane_in[b, n]
             line_across[b, z] = total
@@ -164,8 +170,9 @@
 
     def add_across(a):
         all_of(ACROSS, a).wait_recv()
-        if a == LEVEL_PART:
-            terms, own, others = [plane_across[k] for k in range(16)], of_level(z), early_line
+        if a in LEVEL_PARTS:
+            b = LEVEL_PARTS.index(a)
+            terms, own, others = [plane_across[b, k] for k in range(16)], of_level(z), early_line
         else:
             b = SQUARE_PARTS.index(a)
             terms, own, others = [line_across[b, k] for k in range(8)], of_square(square), early_plane
@@ -179,7 +186,7 @@
 
     def pass_on(a):
         all_of(ROUND, a).wait_recv()
-        here = gathered.at[core, a]
+        here = gathered.at[core, a, pl.ds(0, SIZES[a])]
         copy_of(HALF, a, here, here, sibling).start()
 
     for stage, a in ORDER:
@@ -187,7 +194,7 @@
     gram = None
     for a in range(PARTS):
         all_of(HALF, a).wait_recv()
-        left, right = gathered[0, a], gathered[1, a]
+        left, right = gathered[0, a, : SIZES[a]], gathered[1, a, : SIZES[a]]
         hi, lo = split(jnp.concatenate([left, right], axis=1))
         cross = contract_rows(hi, lo)
         term = contract_rows(hi, hi) + (cross + cross.T)
@@ -196,8 +203,9 @@
     row = device * 4
     b = lax.div(lax.rem(row, 48), 16)
     in_square = lax.div(row, 48) * SQUARE_ROWS + lax.rem(row, 16)
-    part = jnp.where(row < 768, jnp.where(b >= LEVEL_PART, b + 1, b), LEVEL_PART)
-    tile = pl.ds(pl.multiple_of(lax.div(jnp.where(row < 768, in_square, row - 768), 8) * 8, 8), 8)
+    in_level = jnp.maximum(row - 768, 0)
+    part = jnp.where(row < 768, 2 * b, 1 + 2 * lax.div(in_level, 128))
+    tile = pl.ds(pl.multiple_of(lax.div(jnp.where(row < 768, in_square, lax.rem(in_level, 128)), 8) * 8, 8), 8)
     for h in range(2):
         eight = gathered[h, part, tile]
         sketch_out[:, 128 * h : 128 * h + 128] = jnp.where(lax.rem(z, 2) == 0, eight[:4], eight[4:])
@@ -221,15 +229,15 @@
             pltpu.VMEM((1024, 256), BF16),
             pltpu.VMEM((1024, 256), BF16),
             pltpu.VMEM((4, 16, 3, SQUARE_ROWS, 128), BF16),
-            pltpu.VMEM((4, 256, 128), BF16),
+            pltpu.VMEM((4, 2, 128, 128), BF16),
             pltpu.VMEM((PARTS, 256, 128), F32),
             pltpu.VMEM((PARTS, 256, 128), F32),
             pltpu.VMEM((PARTS, 256, 128), F32),
             pltpu.VMEM((1024, 128), F32),
             pltpu.VMEM((3, 15, SQUARE_ROWS, 128), F32),
             pltpu.VMEM((3, 8, SQUARE_ROWS, 128), F32),
-            pltpu.VMEM((7, LEVEL_ROWS, 128), F32),
-            pltpu.VMEM((16, LEVEL_ROWS, 128), F32),
+            pltpu.VMEM((2, 7, LEVEL_ROWS, 128), F32),
+            pltpu.VMEM((2, 16, LEVEL_ROWS, 128), F32),
             pltpu.VMEM((2, PARTS, 256, 128), F32),
             dma((3,)), dma((5,)), dma((5, PARTS)),
         ],

time: 32.5 us -> 32.1 us (0.988)
    pallas_call x1, Pallas kernels: 31 us -> 30.7 us  [on_device(): pl.pallas_call(kernel, out_shape=(pltpu.VMEM((4, 256), F32), pltpu.VMEM((...]
where the time goes in v5:
time: 32.1 us; the launch traced here: 32 us
  Pallas kernels  31.4 us (98%)
  between operations  0.64 us (2%)
    pallas_call x1, Pallas kernels, on_device(): pl.pallas_call(kernel, out_shape=(pltpu.VMEM((4, 256), F32), pltpu.VMEM((...  30.7 us
    pallas_call x1, Pallas kernels, on_device(): pl.pallas_call(hand_out, out_shape=(jax.ShapeDtypeStruct((4, 256), F32),...  0.72 us

profile of v5, /device:TPU:1, one launch (start us, length us, event | category | flops | bytes accessed | tf_op | source)
XLA Modules:
  0.0 32.0 jit_solution(9168834187074441589)
XLA Ops:
  0.6 30.7 %shard_map.50 = (f32[4,256]{1,0:T(4,128)S(1)}, f32[256,256]{1,0:T(8,128)S(1)}) custom-call(f32[1024,256]{1,0:T(8,128)} %design.1, s32[1,1024]{1,0:T(1,128)} %bitcast.2, s32[1,1024]{1,0:T(1,128)} %bitcast.3), custom_call_target="tpu_custom_call" | custom-call | tf_op jit(solution)/shard_map/pallas_call | solution.py:220
  31.3 0.7 %shard_map.51 = (f32[4,256]{1,0:T(4,128)}, f32[256,256]{1,0:T(8,128)}) custom-call(f32[4,256]{1,0:T(4,128)S(1)} %get-tuple-element.4.sketch, f32[256,256]{1,0:T(8,128)S(1)} %get-tuple-element.5.gram), custom_call_target="tpu_custom_call" | custom-call | tf_op jit(solution)/shard_map/pallas_call | solution.py:246

commit v6 on v5

--- a/solution.py
+++ b/solution.py
@@ -44,9 +44,11 @@
     device = wide * 8 + z
     load_ids = pltpu.make_async_copy(ids, ids_in, load_sem.at[0])
     load_ids.start()
-    load = pltpu.make_async_copy(design, rows_in, load_sem.at[1])
-    load.start()
-    load_flips = pltpu.make_async_copy(flips, flips_in, load_sem.at[2])
+    quarters = [pl.ds(256 * k, 256) for k in range(4)]
+    loads = [pltpu.make_async_copy(design.at[q], rows_in.at[q], load_sem.at[2 + k]) for k, q in enumerate(quarters)]
+    for load in loads:
+        load.start()
+    load_flips = pltpu.make_async_copy(flips, flips_in, load_sem.at[1])
     load_flips.start()
 
     squares = [lax.rem(x + dx, 4) * 4 + lax.rem(y + dy, 4) for dx, dy in PLANE]
@@ -88,10 +90,11 @@
 
     load_flips.wait()
     flip = flips_in[...].astype(F32).astype(BF16)
-    load.wait()
-    hi, lo = split(rows_in[...] * (1.0 / 512.0))
-    rows_hi[...] = hi
-    rows_lo[...] = lo
+    for load, q in zip(loads, quarters):
+        load.wait()
+        hi, lo = split(rows_in[q] * (1.0 / 512.0))
+        rows_hi[q] = hi
+        rows_lo[q] = lo
 
     def signs_of(a, j):
         if a in LEVEL_PARTS:
@@ -196,8 +199,7 @@
         all_of(HALF, a).wait_recv()
         left, right = gathered[0, a, : SIZES[a]], gathered[1, a, : SIZES[a]]
         hi, lo = split(jnp.concatenate([left, right], axis=1))
-        cross = contract_rows(hi, lo)
-        term = contract_rows(hi, hi) + (cross + cross.T)
+        term = contract_rows(hi, hi) + (contract_rows(hi, lo) + contract_rows(lo, hi))
         gram = term if gram is None else gram + term
     gram_out[...] = gram * (1.0 / 1024.0)
     row = device * 4
@@ -239,7 +241,7 @@
             pltpu.VMEM((2, 7, LEVEL_ROWS, 128), F32),
             pltpu.VMEM((2, 16, LEVEL_ROWS, 128), F32),
             pltpu.VMEM((2, PARTS, 256, 128), F32),
-            dma((3,)), dma((5,)), dma((5, PARTS)),
+            dma((6,)), dma((5,)), dma((5, PARTS)),
         ],
         compiler_params=pltpu.CompilerParams(collective_id=0, has_side_effects=True, vmem_limit_bytes=40 << 20),
     )(*[pltpu.with_memory_space_constraint(v, pltpu.HBM) for v in (design, sign_flips.reshape(1, 1024), sample_ids.reshape(1, 1024))])

time: 32.1 us -> 32.1 us (level)
  no operation moved by 1% of the time
where the time goes in v6:
time: 32.1 us; the launch traced here: 32 us
  Pallas kernels  31.4 us (98%)
  between operations  0.64 us (2%)
    pallas_call x1, Pallas kernels, on_device(): pl.pallas_call(kernel, out_shape=(pltpu.VMEM((4, 256), F32), pltpu.VMEM((...  30.7 us
    pallas_call x1, Pallas kernels, on_device(): pl.pallas_call(hand_out, out_shape=(jax.ShapeDtypeStruct((4, 256), F32),...  0.72 us

profile of v6, /device:TPU:1, one launch (start us, length us, event | category | flops | bytes accessed | tf_op | source)
XLA Modules:
  0.0 32.0 jit_solution(8250070871613550151)
XLA Ops:
  0.6 30.7 %shard_map.50 = (f32[4,256]{1,0:T(4,128)S(1)}, f32[256,256]{1,0:T(8,128)S(1)}) custom-call(f32[1024,256]{1,0:T(8,128)} %design.1, s32[1,1024]{1,0:T(1,128)} %bitcast.2, s32[1,1024]{1,0:T(1,128)} %bitcast.3), custom_call_target="tpu_custom_call" | custom-call | tf_op jit(solution)/shard_map/pallas_call | solution.py:222
  31.3 0.7 %shard_map.51 = (f32[4,256]{1,0:T(4,128)}, f32[256,256]{1,0:T(8,128)}) custom-call(f32[4,256]{1,0:T(4,128)S(1)} %get-tuple-element.4.sketch, f32[256,256]{1,0:T(8,128)S(1)} %get-tuple-element.5.gram), custom_call_target="tpu_custom_call" | custom-call | tf_op jit(solution)/shard_map/pallas_call | solution.py:248
